TPU v7x, 512 devices: a whole 4x8x8 slice. The times are simulated.
512 devices in a mesh: vec: 16 (over z, y_hi), orb: 32 (over y_lo, x, core).
Axes of the slice: x: 4, y: 8 (y_hi: 2, y_lo: 4; y = y_hi * 4 + y_lo), z: 8, core: 2. Of those that a mesh axis runs over, the one named last changes fastest.
Arguments:
- greens: bfloat16 [256, 144000], P('vec', 'orb'), may hold values from -6 to 6
- cholesky: bfloat16 [8192, 144000], P('vec', 'orb'), may hold values from -0.0625 to 0.0625
- trial_green: bfloat16 [144000], P('orb'), may hold values from -6 to 6
- gaussian: float32 [256, 8192], P('orb', 'vec'), may hold values from -6 to 6
Outputs:
- force_bias: float32 [256, 8192], P('orb', 'vec')
- potential: bfloat16 [256, 144000], P('vec', 'orb')
All inputs are finite; a program needn't handle non-finite values.
Results may differ from a plain program's by a relative error of at most 0.0049.
Values may be sent and summed in bfloat16 or wider, within the bound.
A program may use at most 64 MiB of HBM per device.

v0:
```python
import jax
import jax.numpy as jnp
from jax import lax
from jax.sharding import PartitionSpec as P

sqrt_step = 0.125
cap_bound = 1.0


def local(greens, cholesky, trial_green, gaussian):
    partial_value = lax.dot_general(
        lax.all_gather(greens, "vec", axis=0, tiled=True),
        cholesky,
        (((1,), (1,)), ((), ())),
        preferred_element_type=jnp.float32,
    )
    shift_part = jnp.dot(cholesky, trial_green, preferred_element_type=jnp.float32)
    share_rows = gaussian.shape[0]
    summed_all, mean_shift = lax.psum((partial_value, shift_part), "orb")
    own_bias = lax.dynamic_slice_in_dim(
        summed_all, lax.axis_index("orb") * share_rows, share_rows, 0
    )
    capped = jnp.clip(sqrt_step * (own_bias - mean_shift[None, :]), -cap_bound, cap_bound)
    aux_field = (gaussian - capped).astype(jnp.bfloat16)
    all_fields = lax.all_gather(aux_field, "orb", axis=0, tiled=True)
    walker_rows = greens.shape[0]
    product = jnp.dot(all_fields, cholesky, preferred_element_type=jnp.float32)
    summed_pot = lax.psum(product, "vec")
    own_pot = lax.dynamic_slice_in_dim(
        summed_pot, lax.axis_index("vec") * walker_rows, walker_rows, 0
    )
    return (capped, own_pot.astype(jnp.bfloat16))


def solution(mesh):
    in_specs = (P("vec", "orb"), P("vec", "orb"), P("orb"), P("orb", "vec"))
    out_specs = (P("orb", "vec"), P("vec", "orb"))
    return jax.shard_map(local, mesh=mesh, in_specs=in_specs, out_specs=out_specs, check_vma=False)
```

profile of v0, /device:TPU:56, one launch (start us, length us, event | category | flops | bytes accessed | tf_op | source)
XLA Modules:
  0.0 864.2 jit_solution(9855289325670855202)
XLA Ops:
  7.2 0.0 all-gather.2.cloned.1.call-start
  7.2 0.7 all-gather.2.cloned.1.call-update
  7.9 0.0 copy-start.1
  7.9 0.0 all-reduce.3.cloned.1.call-start
  8.0 110.6 %all-gather.2.cloned.1.call-done = bf16[256,4500]{1,0:T(8,128)(2,1)} async-done(((bf16[16,4500]{1,0:T(8,128)(2,1)}), bf16[256,4500]{1,0:T(8,128)(2,1)}) %all-gather.2.cloned.1.call-update) | async-done | bytes 2304016 | tf_op jit(solution)/shard_map/all_gather | solution.py:12
  118.5 5.2 fusion
  123.7 0.0 copy-start
  123.7 0.0 all-reduce.3.cloned.1.call-update
  123.8 0.0 copy-done.1
  123.8 3.0 fusion.1
  126.8 55.8 %psum.22 = f32[512]{0:T(512)S(1)} all-reduce(f32[512]{0:T(512)S(1)} %bitcast.7), channel_id=1, replica_groups=mesh['vec'=16,'orb'=32] {'orb'}, use_global_device_ids=true, to_apply=%region_1.0 | all-reduce | flops 512 | bytes 4096 | tf_op jit(solution)/shard_map/psum | solution.py:19
  182.6 208.3 %all-reduce.3.cloned.1.call-done = f32[256,512]{1,0:T(8,128)} async-done(((f32[256,512]{1,0:T(8,128)}), f32[256,512]{1,0:T(8,128)}) %all-reduce.3.cloned.1.call-update) | async-done | bytes 524304 | tf_op jit(solution)/shard_map/psum | solution.py:19
  390.9 0.0 copy-done
  390.9 1.3 subtract_convert_fusion
  392.2 46.4 %all_gather.7 = bf16[256,512]{1,0:T(8,128)(2,1)S(1)} all-gather(bf16[8,512]{1,0:T(8,128)(2,1)S(1)} %get-tuple-element.2), channel_id=1, replica_groups=mesh['vec'=16,'orb'=32] {'orb'}, dimensions={0}, use_global_device_ids=true | all-gather | bytes 270336 | tf_op jit(solution)/shard_map/all_gather | solution.py:25
  438.5 5.8 fusion.2
  444.4 412.3 %all-reduce.4 = bf16[256,4500]{1,0:T(8,128)(2,1)S(1)} all-reduce(f32[256,4500]{1,0:T(8,128)} %fusion.2), channel_id=1, replica_groups=mesh['vec'=16,'orb'=32] {'vec'}, use_global_device_ids=true, to_apply=%region_2.3 | all-reduce | flops 1152000 | bytes 6912000 | tf_op jit(solution)/shard_map/psum | solution.py:28
  856.7 0.7 dynamic-slice_convert_fusion
  (1 shorter events, 0.0 us)
Async XLA Ops:
  7.2 111.3 %all-gather.2.cloned.1.call-start = ((), (), s32[]{:S(2)}) async-start(), calls=%async_computation | async-start | bytes 2506752 | tf_op jit(solution)/shard_map/all_gather | solution.py:12
  7.9 115.9 %copy-start.1 = (bf16[4500]{0:T(1024)(128)(2,1)S(1)}, bf16[4500]{0:T(1024)(128)(2,1)}, u32[]{:S(2)}) copy-start(bf16[4500]{0:T(1024)(128)(2,1)} %param.6) | copy-start | bytes 27004
  7.9 382.9 %all-reduce.3.cloned.1.call-start = ((), (), s32[]{:S(2)}) async-start(), calls=%async_computation.1 | async-start | bytes 1048576 | tf_op jit(solution)/shard_map/psum | solution.py:19
  123.7 267.1 %copy-start = (f32[8,512]{1,0:T(8,128)S(1)}, f32[8,512]{1,0:T(8,128)}, u32[]{:S(2)}) copy-start(f32[8,512]{1,0:T(8,128)} %param.7) | copy-start | bytes 49156
Sparse Core Ops, SparseCore 0:
  11.2 107.2 all-gather.1
  123.9 266.9 all-reduce.2
where the time goes:
time: 866 us; the launch traced here: 864 us
  blocking collectives  514 us (59%)
  waiting for transfers between devices  320 us (37%)
  matrix products  14.1 us (2%)
  between operations  14.1 us (2%)
    psum x1, blocking collectives, local(): summed_pot = lax.psum(product, 'vec')  412 us
    psum x1, waiting for transfers between devices, local(): summed_all, mean_shift = lax.psum((partial_value, shift_part), 'orb')  208 us
    all_gather x1, waiting for transfers between devices, local(): lax.all_gather(greens, 'vec', axis=0, tiled=True)  111 us
    psum x1, blocking collectives, local(): summed_all, mean_shift = lax.psum((partial_value, shift_part), 'orb')  55.8 us
    all_gather x1, blocking collectives, local(): all_fields = lax.all_gather(aux_field, 'orb', axis=0, tiled=True)  46.4 us
  transfers between devices with their start and end apart: 2, of which 2 were waited for; matrix products, arithmetic and copies ran while one was open for 0% of the time, Pallas kernels for 0%

commit v1 on v0

v1 whole, which is shorter than its diff:
```python
import functools

import jax
import jax.numpy as jnp
from jax import lax
from jax.experimental import pallas as pl
from jax.experimental.pallas import tpu as pltpu
from jax.sharding import PartitionSpec as P

MESH = pl.DeviceIdType.MESH
sqrt_step = 0.125
cap_bound = 1.0
NZ = 8
NORB = 32
RIGHT = (4, 3)
LEFT = (3, 4)
NT = (((1,), (1,)), ((), ()))
NN = (((1,), (0,)), ((), ()))


def slot(dz, p):
    return (dz % NZ) * 2 + p


def kernel(
    g_hbm, c_hbm, t_ref, n_ref, fb_ref, pot_ref,
    g_all, chol, shift, d_send, d_own, d_recv, n_all, fb_half, fb_both, aux_all, part, p_send, p_recv, y_send, y_recv,
    load_sem, a_send, a_recv, b_send, b_recv, n_sem, f_sem, c_send, c_recv, e_send, e_recv, y_sem,
):
    v, o = lax.axis_index("vec"), lax.axis_index("orb")
    z, yh = v // 2, lax.rem(v, 2)
    half = lax.rem(o, 2)
    right = (lax.rem(z + 1, NZ) * 2 + yh, o)
    left = (lax.rem(z + NZ - 1, NZ) * 2 + yh, o)
    across = (z * 2 + 1 - yh, o)
    mate = (v, o + 1 - 2 * half)

    def send(src, dst, s_sem, r_sem, device):
        return pltpu.make_async_remote_copy(
            src_ref=src, dst_ref=dst, send_sem=s_sem, recv_sem=r_sem, device_id=device, device_id_type=MESH
        )

    def block(dz, p):
        return lax.rem(z + dz % NZ, NZ) * 2 + (yh if p == 0 else 1 - yh)

    load_g = pltpu.make_async_copy(g_hbm, g_all.at[0], load_sem.at[0])
    load_c = pltpu.make_async_copy(c_hbm, chol, load_sem.at[1])
    load_g.start()
    load_c.start()

    barrier = pltpu.get_barrier_semaphore()
    for device in (right, left, across):
        pl.semaphore_signal(barrier, inc=1, device_id=device, device_id_type=MESH)

    def greet(k, _):
        pl.semaphore_signal(barrier, inc=1, device_id=(v, lax.rem(o + k, NORB)), device_id_type=MESH)
        return 0

    lax.fori_loop(1, NORB, greet, 0)
    pl.semaphore_wait(barrier, NORB + 2)

    def a_copy(p, way, step):
        sign = -1 if way == 0 else 1
        return send(
            g_all.at[slot(sign * (step - 1), p)], g_all.at[slot(sign * step, p)],
            a_send.at[p, way, step - 1], a_recv.at[p, way, step - 1], right if way == 0 else left,
        )

    load_g.wait()
    cross = send(g_all.at[0], g_all.at[1], y_sem.at[0], y_sem.at[1], across)
    a_copy(0, 0, 1).start()
    a_copy(0, 1, 1).start()
    cross.start()
    n_copy = send(
        n_ref.at[:, pl.ds(pl.multiple_of((1 - half) * 256, 256), 256)], n_all.at[half], n_sem.at[0], n_sem.at[1], mate
    )
    n_copy.start()
    n_all[half] = n_ref[:, pl.ds(pl.multiple_of(half * 256, 256), 256)]

    def products(entries, extra=None):
        rows = [g_all[slot(dz, p)] for dz, p in entries]
        if extra is not None:
            rows.append(extra)
        prod = lax.dot_general(jnp.concatenate(rows, axis=0), chol[...], NT, preferred_element_type=jnp.float32)
        if extra is not None:
            shift[...] = prod[16 * len(entries) :]
        for i, (dz, p) in enumerate(entries):
            value = prod[16 * i : 16 * i + 16] - shift[...]
            b = block(dz, p)
            for h in range(2):
                s = slot(dz, p) * 2 + h
                d_send[s] = value[:, 256 * h : 256 * h + 256]
                owner = 2 * b + h

                @pl.when(owner != o)
                def _():
                    send(
                        d_send.at[s], d_recv.at[lax.rem(o - owner + NORB, NORB) - 1], b_send, b_recv, (v, owner)
                    ).start()

                @pl.when(owner == o)
                def _():
                    d_own[...] = value[:, 256 * h : 256 * h + 256]

    def pass_on(p, step):
        for way, hops in ((0, RIGHT[p]), (1, LEFT[p])):
            if step <= hops:
                a_copy(p, way, step).wait_recv()
                if step < hops:
                    a_copy(p, way, step + 1).start()

    load_c.wait()
    products([(0, 0)], jnp.broadcast_to(t_ref[...], (16, t_ref.shape[1])))
    pass_on(0, 1)
    products([(-1, 0), (1, 0)])
    cross.wait_recv()
    a_copy(1, 0, 1).start()
    a_copy(1, 1, 1).start()
    pass_on(0, 2)
    products([(0, 1), (-2, 0), (2, 0)])
    pass_on(1, 1)
    pass_on(0, 3)
    products([(-1, 1), (1, 1)])
    products([(-3, 0), (3, 0)])
    pass_on(1, 2)
    pass_on(0, 4)
    products([(-2, 1), (2, 1), (-4, 0)])
    pass_on(1, 3)
    products([(-3, 1), (3, 1)])
    pass_on(1, 4)
    products([(4, 1)])

    n_copy.wait()
    pltpu.make_async_copy(d_recv, d_recv, b_recv).wait()

    def add(k, total):
        return total + d_recv[k]

    total = lax.fori_loop(0, NORB - 1, add, d_own[...])
    capped = jnp.clip(sqrt_step * total, -cap_bound, cap_bound)
    noise = jnp.concatenate([n_all[0], n_all[1]], axis=0)
    aux_all[o] = (noise - capped).astype(jnp.bfloat16)

    def c_copy(k, _):
        send(aux_all.at[o], aux_all.at[o], c_send, c_recv, (v, lax.rem(o + k, NORB))).start()
        return 0

    lax.fori_loop(1, NORB, c_copy, 0)
    fb_half[0] = capped[:8]
    fb_half[1] = capped[8:]
    f_copy = send(fb_half.at[1 - half], fb_both.at[half], f_sem.at[0], f_sem.at[1], mate)
    f_copy.start()
    fb_both[half] = fb_half[half]
    pltpu.make_async_copy(aux_all.at[pl.ds(0, NORB - 1)], aux_all.at[pl.ds(0, NORB - 1)], c_recv).wait()

    def potential(dest, entries):
        rows = []
        for dz, p in entries:
            b = block(dz, p)
            rows.append(jnp.concatenate([aux_all[2 * b], aux_all[2 * b + 1]], axis=1))
        lhs = jnp.concatenate(rows, axis=0)
        width = part.shape[2]
        for j in range(0, width, 512):
            m = min(512, width - j)
            part[dest, : lhs.shape[0], j : j + m] = lax.dot_general(
                lhs, chol[:, j : j + m], NN, preferred_element_type=jnp.float32
            )

    def e_copy(p, way, step):
        i = (p * 2 + way) * 4 + step - 1
        return send(
            p_send.at[i], p_recv.at[i], e_send.at[i], e_recv.at[i], right if way == 0 else left
        )

    def hop(p, step):
        i = 0
        ways = [(w, n) for w, n in ((0, RIGHT[p]), (1, LEFT[p])) if step <= n]
        sign = {0: 1, 1: -1}
        potential(p, [(sign[w] * (n - step + 1), p) for w, n in ways])
        for i, (w, _) in enumerate(ways):
            value = part[p, 16 * i : 16 * i + 16, :]
            if step > 1:
                e_copy(p, w, step - 1).wait_recv()
                value = value + p_recv[(p * 2 + w) * 4 + step - 2].astype(jnp.float32)
            p_send[(p * 2 + w) * 4 + step - 1] = value.astype(jnp.bfloat16)
            e_copy(p, w, step).start()

    def last(p):
        value = part[2, 16 * p : 16 * p + 16, :]
        for w, n in ((0, RIGHT[p]), (1, LEFT[p])):
            e_copy(p, w, n).wait_recv()
            value = value + p_recv[(p * 2 + w) * 4 + n - 1].astype(jnp.float32)
        return value

    for step in (1, 2, 3, 4):
        hop(1, step)
        hop(0, step)
    potential(2, [(0, 0), (0, 1)])
    y_send[...] = last(1).astype(jnp.bfloat16)
    back = send(y_send, y_recv, y_sem.at[2], y_sem.at[3], across)
    back.start()
    mine = last(0)
    f_copy.wait()
    fb_ref[:, :256] = fb_both[0]
    fb_ref[:, 256:] = fb_both[1]
    back.wait_recv()
    pot_ref[...] = (mine + y_recv[...].astype(jnp.float32)).astype(jnp.bfloat16)

    cross.wait_send()
    back.wait_send()
    for p in range(2):
        for way, hops in ((0, RIGHT[p]), (1, LEFT[p])):
            for step in range(1, hops + 1):
                a_copy(p, way, step).wait_send()
                e_copy(p, way, step).wait_send()
    pltpu.make_async_copy(d_recv, d_recv, b_send).wait()
    pltpu.make_async_copy(aux_all.at[pl.ds(0, NORB - 1)], aux_all.at[pl.ds(0, NORB - 1)], c_send).wait()


def local(greens, cholesky, trial_green, gaussian):
    walkers, pairs = greens.shape
    vectors = cholesky.shape[0]
    bf, f4, vm = jnp.bfloat16, jnp.float32, pltpu.VMEM
    dma = pltpu.SemaphoreType.DMA
    return pl.pallas_call(
        kernel,
        out_shape=(
            jax.ShapeDtypeStruct(gaussian.shape, f4),
            jax.ShapeDtypeStruct(greens.shape, bf),
        ),
        in_specs=[pl.BlockSpec(memory_space=pl.ANY)] * 2 + [pl.BlockSpec(memory_space=vm)] * 2,
        out_specs=(pl.BlockSpec(memory_space=vm),) * 2,
        scratch_shapes=[
            vm((2 * NZ, walkers, pairs), bf),
            vm((vectors, pairs), bf),
            vm((walkers, vectors), f4),
            vm((4 * NZ, 16, 256), f4),
            vm((16, 256), f4),
            vm((NORB - 1, 16, 256), f4),
            vm((2, 8, 256), f4),
            vm((2, 8, 256), f4),
            vm((2, 8, 256), f4),
            vm((NORB, 16, 256), bf),
            vm((3, 2 * walkers, pairs), f4),
            vm((16, walkers, pairs), bf),
            vm((16, walkers, pairs), bf),
            vm((walkers, pairs), bf),
            vm((walkers, pairs), bf),
            dma((2,)),
            dma((2, 2, 4)),
            dma((2, 2, 4)),
            dma(()),
            dma(()),
            dma((2,)),
            dma((2,)),
            dma(()),
            dma(()),
            dma((16,)),
            dma((16,)),
            dma((4,)),
        ],
        compiler_params=pltpu.CompilerParams(
            collective_id=0, has_side_effects=True, vmem_limit_bytes=40 << 20
        ),
        cost_estimate=pl.CostEstimate(flops=2400000000, bytes_accessed=5200000, transcendentals=0),
    )(greens, cholesky, trial_green.reshape(1, pairs), gaussian)


def solution(mesh):
    in_specs = (P("vec", "orb"), P("vec", "orb"), P("orb"), P("orb", "vec"))
    out_specs = (P("orb", "vec"), P("vec", "orb"))
    return jax.shard_map(local, mesh=mesh, in_specs=in_specs, out_specs=out_specs, check_vma=False)
```

time: 866 us -> 106 us (0.12)
  blocking collectives: 514 us -> 0 us
  waiting for transfers between devices: 320 us -> 0 us
  Pallas kernels: 0 us -> 94.1 us
  matrix products: 14.1 us -> 0 us
  between operations: 14.1 us -> 0.66 us
  local copies, waits for them, and re-layouts: 0.7 us -> 11.1 us
    psum x2 -> x0, blocking collectives: 468 us -> none  [the longest x1 412 us: local(): summed_pot = lax.psum(product, 'vec')]
    psum x1 -> x0, waiting for transfers between devices: 208 us -> none  [local(): summed_all, mean_shift = lax.psum((partial_value, shift_part), 'orb')]
    all_gather x1 -> x0, waiting for transfers between devices: 111 us -> none  [local(): lax.all_gather(greens, 'vec', axis=0, tiled=True)]
    pallas_call x0 -> x1, Pallas kernels: none -> 94.1 us  [local(): pl.pallas_call(kernel, out_shape=(jax.ShapeDtypeStruct(gaussian.shape, f4...]
    all_gather x1 -> x0, blocking collectives: 46.4 us -> none  [local(): all_fields = lax.all_gather(aux_field, 'orb', axis=0, tiled=True)]
    dot_general x3 -> x0, matrix products: 14.1 us -> none  [the longest x1 5.85 us: local(): product = jnp.dot(all_fields, cholesky, preferred_element_type=jnp.float32)]
    unnamed x5 -> x9, local copies, waits for them, and re-layouts: 0.02 us -> 10.3 us
  transfers between devices with their start and end apart: 2 -> 0, of which waited for: 2 -> 0; matrix products, arithmetic and copies ran while one was open for 0% -> 0% of each run, Pallas kernels for 0% -> 0%
where the time goes in v1:
time: 106 us
  Pallas kernels  94.1 us (89%)
  local copies, waits for them, and re-layouts  11.1 us (10%)
    pallas_call x1, Pallas kernels, local(): pl.pallas_call(kernel, out_shape=(jax.ShapeDtypeStruct(gaussian.shape, f4...  94.1 us
    unnamed x9, local copies, waits for them, and re-layouts  10.3 us

profile of v1, /device:TPU:56, one launch (start us, length us, event | category | flops | bytes accessed | tf_op | source)
XLA Modules:
  0.0 105.9 jit_solution(6772262159814359817)
XLA Ops:
  0.6 0.0 copy-start.2
  0.6 0.0 copy-start.1
  0.6 0.8 reshape.7.t_ref
  1.4 6.7 %copy.6.c_hbm = bf16[512,4500]{1,0:T(8,128)(2,1)} copy(bf16[512,4500]{0,1:T(8,128)(2,1)} %param.5) | data formatting | bytes 9216000 | tf_op args[1]
  8.1 0.0 copy-done.2
  8.1 0.0 copy-done.1
  8.1 0.0 copy-start
  8.1 2.3 %copy-done = bf16[512,4500]{1,0:T(8,128)(2,1)S(1)} copy-done((bf16[512,4500]{1,0:T(8,128)(2,1)S(1)}, bf16[512,4500]{1,0:T(8,128)(2,1)}, u32[]{:S(2)}) %copy-start) | copy-done | bytes 4608024
  10.5 94.1 %shard_map.59 = (f32[8,512]{1,0:T(8,128)S(1)}, bf16[16,4500]{1,0:T(8,128)(2,1)S(1)}) custom-call(bf16[16,4500]{1,0:T(8,128)(2,1)S(1)} %copy-done.1, bf16[512,4500]{1,0:T(8,128)(2,1)S(1)} %copy-done, bf16[1,4500]{1,0:T(2,128)(2,1)S(1)} %reshape.7.t_ref, f32[8,512]{1,0:T(8,128)S(1)} %copy-done.2), custom_call_target="tpu_custom_call" | custom-call | flops 2400000000 | bytes 5200000 | tf_op jit(solution)/shard_map/pallas_call | solution.py:225
  104.6 0.6 copy.9
  105.2 0.7 copy.10
Async XLA Ops:
  0.6 7.5 %copy-start.2 = (f32[8,512]{1,0:T(8,128)S(1)}, f32[8,512]{1,0:T(8,128)}, u32[]{:S(2)}) copy-start(f32[8,512]{1,0:T(8,128)} %n_ref.1) | copy-start | bytes 49156
  0.6 7.5 %copy-start.1 = (bf16[16,4500]{1,0:T(8,128)(2,1)S(1)}, bf16[16,4500]{1,0:T(8,128)(2,1)}, u32[]{:S(2)}) copy-start(bf16[16,4500]{1,0:T(8,128)(2,1)} %g_hbm.1) | copy-start | bytes 432004
  8.1 2.3 %copy-start = (bf16[512,4500]{1,0:T(8,128)(2,1)S(1)}, bf16[512,4500]{1,0:T(8,128)(2,1)}, u32[]{:S(2)}) copy-start(bf16[512,4500]{1,0:T(8,128)(2,1)} %copy.6.c_hbm) | copy-start | bytes 13824004

commit v2 on v0

v2 whole, which is shorter than its diff:
```python
import jax
import jax.numpy as jnp
from jax import lax
from jax.experimental import pallas as pl
from jax.experimental.pallas import tpu as pltpu
from jax.sharding import PartitionSpec as P

MESH = pl.DeviceIdType.MESH
sqrt_step = 0.125
cap_bound = 1.0
NZ = 8
NORB = 32
PAIRS = 4500
WIDE = 1536
NC = -(-PAIRS // WIDE)
WIDTHS = [min(WIDE, PAIRS - WIDE * c) for c in range(NC)]
HOPS = ((4, 3), (3, 4))
NT = (((1,), (1,)), ((), ()))
NN = (((1,), (0,)), ((), ()))


def slot(dz, p):
    return (dz % NZ) * 2 + p


def kernel(
    g_in, c_hbm, t_ref, n_ref, fb_ref, pot_ref,
    g_all, chol, shift, d_send, d_own, d_recv, n_all, fb_half, fb_both, aux_all, p_send, p_recv, y_send, y_recv,
    load_sem, a_send, a_recv, b_send, b_recv, n_sem, f_sem, c_send, c_recv, e_send, e_recv, y_sem, y_back,
):
    v, o = lax.axis_index("vec"), lax.axis_index("orb")
    z, yh = v // 2, lax.rem(v, 2)
    half = lax.rem(o, 2)
    kind = jnp.where(lax.rem(o // 2, 2) == yh, 0, 1)
    sides = ((lax.rem(z + 1, NZ) * 2 + yh, o), (lax.rem(z + NZ - 1, NZ) * 2 + yh, o))
    across = (z * 2 + 1 - yh, o)
    mate = (v, o + 1 - 2 * half)

    def send(src, dst, s_sem, r_sem, device):
        return pltpu.make_async_remote_copy(
            src_ref=src, dst_ref=dst, send_sem=s_sem, recv_sem=r_sem, device_id=device, device_id_type=MESH
        )

    def block(dz, p):
        return lax.rem(z + dz % NZ, NZ) * 2 + (yh if p == 0 else 1 - yh)

    load_c = pltpu.make_async_copy(c_hbm, chol, load_sem)
    barrier = pltpu.get_barrier_semaphore()
    for device in (*sides, across):
        pl.semaphore_signal(barrier, inc=1, device_id=device, device_id_type=MESH)

    def greet(k, _):
        pl.semaphore_signal(barrier, inc=1, device_id=(v, lax.rem(o + k, NORB)), device_id_type=MESH)
        return 0

    lax.fori_loop(1, NORB, greet, 0)
    load_c.start()

    if WIDTHS[-1] != WIDE:
        g_all[0, NC - 1] = jnp.zeros((16, WIDE), jnp.bfloat16)
    for c in range(NC):
        g_all[0, c, :, : WIDTHS[c]] = g_in[:, WIDE * c : WIDE * c + WIDTHS[c]]
    pl.semaphore_wait(barrier, NORB + 2)

    def a_copy(p, way, step, c):
        sign = 1 if way else -1
        i = ((p * 2 + way) * 4 + step - 1) * NC + c
        return send(
            g_all.at[slot(sign * (step - 1), p), c], g_all.at[slot(sign * step, p), c], a_send.at[i], a_recv.at[i], sides[way]
        )

    def cross(c):
        return send(g_all.at[0, c], g_all.at[1, c], y_sem.at[0, c], y_sem.at[1, c], across)

    for c in range(NC):
        a_copy(0, 0, 1, c).start()
        a_copy(0, 1, 1, c).start()
    for c in range(NC):
        cross(c).start()
    n_copy = send(
        n_ref.at[:, pl.ds(pl.multiple_of((1 - half) * 256, 256), 256)], n_all.at[half], n_sem.at[0], n_sem.at[1], mate
    )
    n_copy.start()
    n_all[half] = n_ref[:, pl.ds(pl.multiple_of(half * 256, 256), 256)]

    def product(lhs, c):
        return lax.dot_general(
            lhs, chol[WIDE * c : WIDE * c + WIDTHS[c], :], NN, preferred_element_type=jnp.float32
        )

    def rows(entries, c):
        return jnp.concatenate([g_all[slot(dz, p), c, :, : WIDTHS[c]] for dz, p in entries], axis=0)

    def to_owners(entries, prod):
        for i, (dz, p) in enumerate(entries):
            value = prod[16 * i : 16 * i + 16] - shift[...]
            b = block(dz, p)
            for h in range(2):
                s = slot(dz, p) * 2 + h
                d_send[s] = value[:, 256 * h : 256 * h + 256]
                owner = 2 * b + h

                @pl.when(owner != o)
                def _():
                    send(
                        d_send.at[s], d_recv.at[lax.rem(o - owner + NORB, NORB) - 1], b_send, b_recv, (v, owner)
                    ).start()

                @pl.when(owner == o)
                def _():
                    d_own[...] = value[:, 256 * h : 256 * h + 256]

    def gather(p, step, more=()):
        ways = [w for w in range(2) if step <= HOPS[p][w]]
        entries = [((step if w else -step), p) for w in ways] + list(more)
        prod = None
        for c in range(NC):
            for w in ways:
                a_copy(p, w, step, c).wait_recv()
                if step < HOPS[p][w]:
                    a_copy(p, w, step + 1, c).start()
            term = product(rows(entries, c), c)
            prod = term if prod is None else prod + term
        to_owners(entries, prod)

    def fields():
        n_copy.wait_recv()
        pltpu.make_async_copy(d_recv, d_recv, b_recv).wait()
        total = lax.fori_loop(0, NORB - 1, lambda k, t: t + d_recv[k], d_own[...])
        capped = jnp.clip(sqrt_step * total, -cap_bound, cap_bound)
        noise = jnp.concatenate([n_all[0], n_all[1]], axis=0)
        aux_all[o] = (noise - capped).astype(jnp.bfloat16)

        def c_copy(k, _):
            send(aux_all.at[o], aux_all.at[o], c_send, c_recv.at[kind], (v, lax.rem(o + k, NORB))).start()
            return 0

        lax.fori_loop(1, NORB, c_copy, 0)
        fb_half[0] = capped[:8]
        fb_half[1] = capped[8:]
        send(fb_half.at[1 - half], fb_both.at[half], f_sem.at[0], f_sem.at[1], mate).start()
        fb_both[half] = fb_half[half]

    def fields_there(p):
        for n, is_own in ((15, kind == p), (16, kind != p)):

            @pl.when(is_own)
            def _():
                pltpu.make_async_copy(aux_all.at[pl.ds(0, n)], aux_all.at[pl.ds(0, n)], c_recv.at[p]).wait()

    load_c.wait()
    first = None
    for c in range(NC):
        trial = jnp.broadcast_to(t_ref[WIDE * c : WIDE * c + WIDTHS[c]][None, :], (16, WIDTHS[c]))
        term = product(jnp.concatenate([rows([(0, 0)], c), trial], axis=0), c)
        first = term if first is None else first + term
    shift[...] = first[16:]
    to_owners([(0, 0)], first[:16])
    gather(0, 1)
    gather(0, 2)
    for c in range(NC):
        cross(c).wait_recv()
        a_copy(1, 1, 1, c).start()
    gather(0, 3)
    for c in range(NC):
        a_copy(1, 0, 1, c).start()
    gather(0, 4, [(0, 1)])
    gather(1, 1)

    @pl.when(kind == 0)
    def _():
        fields()

    gather(1, 2)
    gather(1, 3)
    gather(1, 4)

    def fields_of(entries):
        parts = []
        for dz, p in entries:
            b = block(dz, p)
            parts.append(jnp.concatenate([aux_all[2 * b], aux_all[2 * b + 1]], axis=1))
        return jnp.concatenate(parts, axis=0)

    def potential(lhs, c):
        return lax.dot_general(lhs, chol[WIDE * c : WIDE * c + WIDTHS[c], :], NT, preferred_element_type=jnp.float32)

    def e_index(p, way, step):
        return (p * 2 + way) * 4 + step - 1

    def e_copy(p, way, step, c):
        i = e_index(p, way, step)
        return send(p_send.at[i, c], p_recv.at[i, c], e_send.at[i * NC + c], e_recv.at[i * NC + c], sides[way])

    def arrived(p, way, step, c):
        e_copy(p, way, step, c).wait_recv()
        return p_recv[e_index(p, way, step), c, :, : WIDTHS[c]].astype(jnp.float32)

    def hop(p, step):
        ways = [w for w in range(2) if step <= HOPS[p][w]]
        lhs = fields_of([((1 - 2 * w) * (HOPS[p][w] - step + 1), p) for w in ways])
        for c in range(NC):
            value = potential(lhs, c)
            for i, w in enumerate(ways):
                own = value[16 * i : 16 * i + 16]
                if step > 1:
                    own = own + arrived(p, w, step - 1, c)
                p_send[e_index(p, w, step), c, :, : WIDTHS[c]] = own.astype(jnp.bfloat16)
                e_copy(p, w, step, c).start()

    def back(c):
        return send(y_send.at[c], y_recv.at[c], y_back.at[0, c], y_back.at[1, c], across)

    fields_there(0)
    hop(0, 1)

    @pl.when(kind == 1)
    def _():
        fields()

    hop(0, 2)
    fields_there(1)
    hop(1, 1)
    hop(1, 2)
    hop(1, 3)
    hop(1, 4)
    hop(0, 3)
    lhs = fields_of([(0, 1)])
    for c in range(NC):
        value = potential(lhs, c)
        for w in range(2):
            value = value + arrived(1, w, HOPS[1][w], c)
        y_send[c, :, : WIDTHS[c]] = value.astype(jnp.bfloat16)
        back(c).start()
    hop(0, 4)
    send(fb_half.at[1 - half], fb_both.at[half], f_sem.at[0], f_sem.at[1], mate).wait()
    fb_ref[:, :256] = fb_both[0]
    fb_ref[:, 256:] = fb_both[1]
    lhs = fields_of([(0, 0)])
    for c in range(NC):
        value = potential(lhs, c)
        for w in range(2):
            value = value + arrived(0, w, HOPS[0][w], c)
        back(c).wait_recv()
        value = value + y_recv[c, :, : WIDTHS[c]].astype(jnp.float32)
        pot_ref[:, WIDE * c : WIDE * c + WIDTHS[c]] = value.astype(jnp.bfloat16)

    n_copy.wait_send()
    for c in range(NC):
        cross(c).wait_send()
        back(c).wait_send()
        for p in range(2):
            for way in range(2):
                for step in range(1, HOPS[p][way] + 1):
                    a_copy(p, way, step, c).wait_send()
                    e_copy(p, way, step, c).wait_send()
    pltpu.make_async_copy(d_recv, d_recv, b_send).wait()
    pltpu.make_async_copy(aux_all.at[pl.ds(0, NORB - 1)], aux_all.at[pl.ds(0, NORB - 1)], c_send).wait()


def local(greens, cholesky, trial_green, gaussian):
    walkers, pairs = greens.shape
    vectors = cholesky.shape[0]
    bf, f4, vm = jnp.bfloat16, jnp.float32, pltpu.VMEM
    dma = pltpu.SemaphoreType.DMA
    return pl.pallas_call(
        kernel,
        out_shape=(
            jax.ShapeDtypeStruct(gaussian.shape, f4),
            jax.ShapeDtypeStruct(greens.shape, bf),
        ),
        in_specs=[pl.BlockSpec(memory_space=m) for m in (vm, pl.ANY, vm, vm)],
        out_specs=(pl.BlockSpec(memory_space=vm),) * 2,
        scratch_shapes=[
            vm((2 * NZ, NC, walkers, WIDE), bf),
            vm((pairs, vectors), bf),
            vm((walkers, vectors), f4),
            vm((4 * NZ, 16, 256), f4),
            vm((16, 256), f4),
            vm((NORB - 1, 16, 256), f4),
            vm((2, 8, 256), f4),
            vm((2, 8, 256), f4),
            vm((2, 8, 256), f4),
            vm((NORB, 16, 256), bf),
            vm((16, NC, walkers, WIDE), bf),
            vm((16, NC, walkers, WIDE), bf),
            vm((NC, walkers, WIDE), bf),
            vm((NC, walkers, WIDE), bf),
            dma(()),
            dma((16 * NC,)),
            dma((16 * NC,)),
            dma(()),
            dma(()),
            dma((2,)),
            dma((2,)),
            dma(()),
            dma((2,)),
            dma((16 * NC,)),
            dma((16 * NC,)),
            dma((2, NC)),
            dma((2, NC)),
        ],
        compiler_params=pltpu.CompilerParams(
            collective_id=0, has_side_effects=True, vmem_limit_bytes=50 << 20
        ),
        cost_estimate=pl.CostEstimate(flops=2400000000, bytes_accessed=5200000, transcendentals=0),
    )(greens, cholesky.T, trial_green, gaussian)


def solution(mesh):
    in_specs = (P("vec", "orb"), P("vec", "orb"), P("orb"), P("orb", "vec"))
    out_specs = (P("orb", "vec"), P("vec", "orb"))
    return jax.shard_map(local, mesh=mesh, in_specs=in_specs, out_specs=out_specs, check_vma=False)
```

time: 866 us -> 90.6 us (0.10)
  the two profiles are of different devices: /device:TPU:56 before, /device:TPU:24 now
where the time goes in v2:
time: 90.6 us; the launch traced here: 90.3 us
  Pallas kernels  86.1 us (95%)
  local copies, waits for them, and re-layouts  3.59 us (4%)
    pallas_call x1, Pallas kernels, local(): pl.pallas_call(kernel, out_shape=(jax.ShapeDtypeStruct(gaussian.shape, f4...  86.1 us
    unnamed x8, local copies, waits for them, and re-layouts  3.59 us

profile of v2, /device:TPU:24, one launch (start us, length us, event | category | flops | bytes accessed | tf_op | source)
XLA Modules:
  0.0 90.3 jit_solution(8377683766854776932)
XLA Ops:
  0.6 0.0 copy-start
  0.6 0.9 copy-done
  1.5 0.0 copy-start.1
  1.5 0.7 copy-done.1
  2.3 0.0 copy-start.2
  2.3 0.7 copy-done.2
  3.0 86.1 %shard_map.59 = (f32[8,512]{1,0:T(8,128)S(1)}, bf16[16,4500]{1,0:T(8,128)(2,1)S(1)}) custom-call(bf16[16,4500]{1,0:T(8,128)(2,1)S(1)} %copy-done, bf16[4500,512]{1,0:T(8,128)(2,1)} %bitcast.1, bf16[4500]{0:T(1024)(128)(2,1)S(1)} %copy-done.2, f32[8,512]{1,0:T(8,128)S(1)} %copy-done.1), custom_call_target="tpu_custom_call" | custom-call | flops 2400000000 | bytes 5200000 | tf_op jit(solution)/shard_map/pallas_call | solution.py:266
  89.0 0.6 copy.8
  89.6 0.7 copy.9
Async XLA Ops:
  0.6 0.9 %copy-start = (bf16[16,4500]{1,0:T(8,128)(2,1)S(1)}, bf16[16,4500]{1,0:T(8,128)(2,1)}, u32[]{:S(2)}) copy-start(bf16[16,4500]{1,0:T(8,128)(2,1)} %g_in.1) | copy-start | bytes 432004
  1.5 0.7 copy-start.1
  2.3 0.7 copy-start.2

commit v3 on v2

--- a/solution.py
+++ b/solution.py
@@ -25,8 +25,8 @@
 
 def kernel(
     g_in, c_hbm, t_ref, n_ref, fb_ref, pot_ref,
-    g_all, chol, shift, d_send, d_own, d_recv, n_all, fb_half, fb_both, aux_all, p_send, p_recv, y_send, y_recv,
-    load_sem, a_send, a_recv, b_send, b_recv, n_sem, f_sem, c_send, c_recv, e_send, e_recv, y_sem, y_back,
+    g_all, chol, shift, keep, m_send, m_recv, d_send, w_send, d_own, d_recv, w_recv, n_all, fb_half, fb_both, aux_all, p_send, p_recv, y_send, y_recv,
+    load_sem, a_send, a_recv, m_out, m_in, b_send, b_recv, n_sem, f_sem, c_send, c_recv, t_send, t_recv, e_send, e_recv, y_sem, y_back,
 ):
     v, o = lax.axis_index("vec"), lax.axis_index("orb")
     z, yh = v // 2, lax.rem(v, 2)
@@ -46,21 +46,21 @@
 
     load_c = pltpu.make_async_copy(c_hbm, chol, load_sem)
     barrier = pltpu.get_barrier_semaphore()
-    for device in (*sides, across):
+    for device in (*sides, across, mate):
         pl.semaphore_signal(barrier, inc=1, device_id=device, device_id_type=MESH)
 
     def greet(k, _):
-        pl.semaphore_signal(barrier, inc=1, device_id=(v, lax.rem(o + k, NORB)), device_id_type=MESH)
+        pl.semaphore_signal(barrier, inc=1, device_id=(v, lax.rem(o + 2 * k, NORB)), device_id_type=MESH)
         return 0
 
-    lax.fori_loop(1, NORB, greet, 0)
+    lax.fori_loop(1, NORB // 2, greet, 0)
     load_c.start()
 
     if WIDTHS[-1] != WIDE:
         g_all[0, NC - 1] = jnp.zeros((16, WIDE), jnp.bfloat16)
     for c in range(NC):
         g_all[0, c, :, : WIDTHS[c]] = g_in[:, WIDE * c : WIDE * c + WIDTHS[c]]
-    pl.semaphore_wait(barrier, NORB + 2)
+    pl.semaphore_wait(barrier, NORB // 2 + 3)
 
     def a_copy(p, way, step, c):
         sign = 1 if way else -1
@@ -75,7 +75,6 @@
     for c in range(NC):
         a_copy(0, 0, 1, c).start()
         a_copy(0, 1, 1, c).start()
-    for c in range(NC):
         cross(c).start()
     n_copy = send(
         n_ref.at[:, pl.ds(pl.multiple_of((1 - half) * 256, 256), 256)], n_all.at[half], n_sem.at[0], n_sem.at[1], mate
@@ -91,26 +90,36 @@
     def rows(entries, c):
         return jnp.concatenate([g_all[slot(dz, p), c, :, : WIDTHS[c]] for dz, p in entries], axis=0)
 
-    def to_owners(entries, prod):
+    def pair_copy(dz, p):
+        i = slot(dz, p)
+        return send(m_send.at[i], m_recv.at[i], m_out.at[i], m_in.at[i], mate)
+
+    def to_mate(entries, prod):
         for i, (dz, p) in enumerate(entries):
             value = prod[16 * i : 16 * i + 16] - shift[...]
+            low, high = value[:, :256], value[:, 256:]
+            keep[slot(dz, p)] = jnp.where(half == 0, low, high)
+            m_send[slot(dz, p)] = jnp.where(half == 0, high, low)
+            pair_copy(dz, p).start()
+
+    def to_owners(entries):
+        for dz, p in entries:
+            pair_copy(dz, p).wait_recv()
+            total = keep[slot(dz, p)] + m_recv[slot(dz, p)]
             b = block(dz, p)
-            for h in range(2):
-                s = slot(dz, p) * 2 + h
-                d_send[s] = value[:, 256 * h : 256 * h + 256]
-                owner = 2 * b + h
-
-                @pl.when(owner != o)
-                def _():
-                    send(
-                        d_send.at[s], d_recv.at[lax.rem(o - owner + NORB, NORB) - 1], b_send, b_recv, (v, owner)
-                    ).start()
-
-                @pl.when(owner == o)
-                def _():
-                    d_own[...] = value[:, 256 * h : 256 * h + 256]
-
-    def gather(p, step, more=()):
+            out, into = ((d_send, d_recv), (w_send, w_recv))[p]
+            out[dz % NZ] = total.astype(out.dtype)
+            place = lax.rem(o // 2 - b + 16, 16)
+
+            @pl.when(place != 0)
+            def _():
+                send(out.at[dz % NZ], into.at[place - 1], b_send.at[p], b_recv.at[p], (v, 2 * b + half)).start()
+
+            @pl.when(place == 0)
+            def _():
+                d_own[...] = total
+
+    def gather(p, step, more=(), before=(), first=False):
         ways = [w for w in range(2) if step <= HOPS[p][w]]
         entries = [((step if w else -step), p) for w in ways] + list(more)
         prod = None
@@ -119,67 +128,83 @@
                 a_copy(p, w, step, c).wait_recv()
                 if step < HOPS[p][w]:
                     a_copy(p, w, step + 1, c).start()
-            term = product(rows(entries, c), c)
+            if c == 0:
+                to_owners(before)
+            lhs = rows(entries, c)
+            if first:
+                trial = t_ref[WIDE * c : WIDE * c + WIDTHS[c]][None, :]
+                lhs = jnp.concatenate([lhs, jnp.broadcast_to(trial, (16, WIDTHS[c]))], axis=0)
+                if c == 0:
+                    load_c.wait()
+            term = product(lhs, c)
             prod = term if prod is None else prod + term
-        to_owners(entries, prod)
-
-    def fields():
+        if first:
+            shift[...] = prod[16 * len(entries) :]
+        to_mate(entries, prod)
+        return entries
+
+    def fields(p):
         n_copy.wait_recv()
-        pltpu.make_async_copy(d_recv, d_recv, b_recv).wait()
-        total = lax.fori_loop(0, NORB - 1, lambda k, t: t + d_recv[k], d_own[...])
+        into = (d_recv, w_recv)[p]
+        pltpu.make_async_copy(into, into, b_recv.at[p]).wait()
+        total = d_own[...]
+        for k in range(15):
+            total = total + into[k].astype(jnp.float32)
         capped = jnp.clip(sqrt_step * total, -cap_bound, cap_bound)
         noise = jnp.concatenate([n_all[0], n_all[1]], axis=0)
-        aux_all[o] = (noise - capped).astype(jnp.bfloat16)
+        mine = aux_all.at[half, lax.rem(o // 2, 2), o // 4]
+        mine[...] = (noise - capped).astype(jnp.bfloat16)
 
         def c_copy(k, _):
-            send(aux_all.at[o], aux_all.at[o], c_send, c_recv.at[kind], (v, lax.rem(o + k, NORB))).start()
+            send(mine, mine, c_send, c_recv.at[p], (v, lax.rem(o + 2 * k, NORB))).start()
             return 0
 
-        lax.fori_loop(1, NORB, c_copy, 0)
+        lax.fori_loop(1, NORB // 2, c_copy, 0)
         fb_half[0] = capped[:8]
         fb_half[1] = capped[8:]
         send(fb_half.at[1 - half], fb_both.at[half], f_sem.at[0], f_sem.at[1], mate).start()
         fb_both[half] = fb_half[half]
 
-    def fields_there(p):
-        for n, is_own in ((15, kind == p), (16, kind != p)):
+    def turn(p):
+        half_fields = aux_all.at[half, yh if p == 0 else 1 - yh]
+        return send(half_fields, half_fields, t_send.at[p], t_recv.at[p], mate)
+
+    def to_turn(p):
+        for n, is_own in ((7, kind == p), (8, kind != p)):
 
             @pl.when(is_own)
             def _():
-                pltpu.make_async_copy(aux_all.at[pl.ds(0, n)], aux_all.at[pl.ds(0, n)], c_recv.at[p]).wait()
-
-    load_c.wait()
-    first = None
-    for c in range(NC):
-        trial = jnp.broadcast_to(t_ref[WIDE * c : WIDE * c + WIDTHS[c]][None, :], (16, WIDTHS[c]))
-        term = product(jnp.concatenate([rows([(0, 0)], c), trial], axis=0), c)
-        first = term if first is None else first + term
-    shift[...] = first[16:]
-    to_owners([(0, 0)], first[:16])
-    gather(0, 1)
-    gather(0, 2)
+                pltpu.make_async_copy(aux_all.at[0, 0, pl.ds(0, n)], aux_all.at[0, 0, pl.ds(0, n)], c_recv.at[p]).wait()
+
+        turn(p).start()
+
+    done = gather(0, 1, [(0, 0)], first=True)
+    done = gather(0, 2, before=done)
     for c in range(NC):
         cross(c).wait_recv()
         a_copy(1, 1, 1, c).start()
-    gather(0, 3)
+    done = gather(0, 3, before=done)
     for c in range(NC):
         a_copy(1, 0, 1, c).start()
-    gather(0, 4, [(0, 1)])
-    gather(1, 1)
+    done = gather(0, 4, [(0, 1)], before=done)
+    done = gather(1, 1, before=done)
 
     @pl.when(kind == 0)
     def _():
-        fields()
-
-    gather(1, 2)
-    gather(1, 3)
-    gather(1, 4)
+        fields(0)
+
+
+    done = gather(1, 2, before=done)
+
+    done = gather(1, 3, before=done)
+    to_turn(0)
+    done = gather(1, 4, before=done)
 
     def fields_of(entries):
         parts = []
         for dz, p in entries:
-            b = block(dz, p)
-            parts.append(jnp.concatenate([aux_all[2 * b], aux_all[2 * b + 1]], axis=1))
+            q, at = (yh if p == 0 else 1 - yh), lax.rem(z + dz % NZ, NZ)
+            parts.append(jnp.concatenate([aux_all[0, q, at], aux_all[1, q, at]], axis=1))
         return jnp.concatenate(parts, axis=0)
 
     def potential(lhs, c):
@@ -211,20 +236,22 @@
     def back(c):
         return send(y_send.at[c], y_recv.at[c], y_back.at[0, c], y_back.at[1, c], across)
 
-    fields_there(0)
+    turn(0).wait_recv()
     hop(0, 1)
+    to_owners(done)
 
     @pl.when(kind == 1)
     def _():
-        fields()
+        fields(1)
 
     hop(0, 2)
-    fields_there(1)
+    to_turn(1)
+    hop(0, 3)
+    turn(1).wait_recv()
     hop(1, 1)
     hop(1, 2)
     hop(1, 3)
     hop(1, 4)
-    hop(0, 3)
     lhs = fields_of([(0, 1)])
     for c in range(NC):
         value = potential(lhs, c)
@@ -254,8 +281,18 @@
                 for step in range(1, HOPS[p][way] + 1):
                     a_copy(p, way, step, c).wait_send()
                     e_copy(p, way, step, c).wait_send()
-    pltpu.make_async_copy(d_recv, d_recv, b_send).wait()
-    pltpu.make_async_copy(aux_all.at[pl.ds(0, NORB - 1)], aux_all.at[pl.ds(0, NORB - 1)], c_send).wait()
+    for p, buffer in enumerate((d_send, w_send)):
+        for n, is_own in ((7, kind == p), (8, kind != p)):
+
+            @pl.when(is_own)
+            def _():
+                pltpu.make_async_copy(buffer.at[pl.ds(0, n)], buffer.at[pl.ds(0, n)], b_send.at[p]).wait()
+
+        for dz in range(NZ):
+            pair_copy(dz, p).wait_send()
+    pltpu.make_async_copy(w_recv, w_recv, c_send).wait()
+    turn(0).wait_send()
+    turn(1).wait_send()
 
 
 def local(greens, cholesky, trial_green, gaussian):
@@ -275,13 +312,18 @@
             vm((2 * NZ, NC, walkers, WIDE), bf),
             vm((pairs, vectors), bf),
             vm((walkers, vectors), f4),
-            vm((4 * NZ, 16, 256), f4),
+            vm((2 * NZ, 16, 256), f4),
+            vm((2 * NZ, 16, 256), f4),
+            vm((2 * NZ, 16, 256), f4),
+            vm((NZ, 16, 256), f4),
+            vm((NZ, 16, 256), bf),
             vm((16, 256), f4),
-            vm((NORB - 1, 16, 256), f4),
+            vm((NORB // 2 - 1, 16, 256), f4),
+            vm((NORB // 2 - 1, 16, 256), bf),
             vm((2, 8, 256), f4),
             vm((2, 8, 256), f4),
             vm((2, 8, 256), f4),
-            vm((NORB, 16, 256), bf),
+            vm((2, 2, NZ, 16, 256), bf),
             vm((16, NC, walkers, WIDE), bf),
             vm((16, NC, walkers, WIDE), bf),
             vm((NC, walkers, WIDE), bf),
@@ -289,11 +331,15 @@
             dma(()),
             dma((16 * NC,)),
             dma((16 * NC,)),
+            dma((2 * NZ,)),
+            dma((2 * NZ,)),
+            dma((2,)),
+            dma((2,)),
+            dma((2,)),
+            dma((2,)),
             dma(()),
-            dma(()),
-            dma((2,)),
-            dma((2,)),
-            dma(()),
+            dma((2,)),
+            dma((2,)),
             dma((2,)),
             dma((16 * NC,)),
             dma((16 * NC,)),

time: 90.6 us -> 90.4 us (level)
  the two profiles are of different devices: /device:TPU:24 before, /device:TPU:56 now
where the time goes in v3:
time: 90.4 us; the launch traced here: 90 us
  Pallas kernels  85.8 us (95%)
  local copies, waits for them, and re-layouts  3.59 us (4%)
    pallas_call x1, Pallas kernels, local(): pl.pallas_call(kernel, out_shape=(jax.ShapeDtypeStruct(gaussian.shape, f4...  85.8 us
    unnamed x8, local copies, waits for them, and re-layouts  3.59 us

profile of v3, /device:TPU:56, one launch (start us, length us, event | category | flops | bytes accessed | tf_op | source)
XLA Modules:
  0.0 90.0 jit_solution(7769438620511765083)
XLA Ops:
  0.6 0.0 copy-start
  0.6 0.9 %copy-done = bf16[16,4500]{1,0:T(8,128)(2,1)S(1)} copy-done((bf16[16,4500]{1,0:T(8,128)(2,1)S(1)}, bf16[16,4500]{1,0:T(8,128)(2,1)}, u32[]{:S(2)}) %copy-start) | copy-done | bytes 144024
  1.5 0.0 copy-start.1
  1.5 0.7 copy-done.1
  2.3 0.0 copy-start.2
  2.3 0.7 copy-done.2
  3.0 85.8 %shard_map.59 = (f32[8,512]{1,0:T(8,128)S(1)}, bf16[16,4500]{1,0:T(8,128)(2,1)S(1)}) custom-call(bf16[16,4500]{1,0:T(8,128)(2,1)S(1)} %copy-done, bf16[4500,512]{1,0:T(8,128)(2,1)} %bitcast.1, bf16[4500]{0:T(1024)(128)(2,1)S(1)} %copy-done.2, f32[8,512]{1,0:T(8,128)S(1)} %copy-done.1), custom_call_target="tpu_custom_call" | custom-call | flops 2400000000 | bytes 5200000 | tf_op jit(solution)/shard_map/pallas_call | solution.py:303
  88.8 0.6 copy.8
  89.4 0.7 copy.9
Async XLA Ops:
  0.6 0.9 %copy-start = (bf16[16,4500]{1,0:T(8,128)(2,1)S(1)}, bf16[16,4500]{1,0:T(8,128)(2,1)}, u32[]{:S(2)}) copy-start(bf16[16,4500]{1,0:T(8,128)(2,1)} %g_in.1) | copy-start | bytes 432004
  1.5 0.7 copy-start.1
  2.3 0.7 copy-start.2
